TPU v7x, 512 devices: a whole 4x8x8 slice. The times are simulated.
512 devices in a mesh: cell: 8 (over z), donor: 8 (over x, core), gene: 8 (over y).
Axes of the slice: x: 4, y: 8, z: 8, core: 2. Of those that a mesh axis runs over, the one named last changes fastest.
Arguments:
- counts: int32 [32768, 2048], P(('cell', 'donor'), 'gene'), may hold values from 0 to 35
- cell_donor: int32 [32768], P(('cell', 'donor')), may hold values from 0 to 511, as said below
- cell_type: int32 [32768], P(('cell', 'donor')), may hold values from -1 to 23, as said below
- covariates: float32 [512, 50], P(('cell', 'donor')), may hold values from -6 to 6
- dosage: int32 [8192, 512], P('gene'), may hold values from 0 to 2
- windows: int32 [2048, 1024], P(('gene', 'cell', 'donor')), may hold values from -1 to 8191, as said below
Outputs:
- association: float32 [24, 2048, 1024], P(None, ('gene', 'cell', 'donor'))
Inputs may be any that keep to these rules, and one draw needn't show every extreme that they name: `cell_donor`: rows come in blocks of 512: a row of block b names a donor d with (d // 8) % 8 = b % 8. Every donor has at least one cell of every cell type. `cell_type`: in each block of 512 rows the live slots (type 0 or more) come first and the empty ones (-1) last; the number of live slots varies from block to block and some block is full. `windows`: row j lists consecutive SNP numbers in ascending order, then -1 to its end; all of them lie in [b * 1024, (b + 1) * 1024) with b = j // 256. A window holds 512 to 1024 SNPs, some window holds exactly 1024, and the last gene's window ends at the last SNP.
All inputs are finite; a program needn't handle non-finite values.
Results may differ from a plain program's by a relative error of at most 0.00045.
Values sent between devices are 32-bit elements; how exact they have to be, the bound alone decides.
No kernel may reach another device: no remote copies, remote signals or barrier semaphores. Data moves between devices by JAX's collectives and lax.ppermute only.
A program may use at most 64 MiB of HBM per device.

v0:
```python
import math
import jax
import jax.numpy as jnp
from jax import lax
from jax.sharding import PartitionSpec as P

CT = 24


def log_cpm(pseudobulk, library):
    return jnp.log2((pseudobulk + 0.5) / (library + 1.0) * 1000000.0)


def with_intercept(covariates):
    intercept = jnp.ones((covariates.shape[0], 1), jnp.float32)
    return jnp.concatenate([intercept, covariates], axis=1)


def factor_lower(gram_sum):
    order = gram_sum.shape[0]
    factor = jnp.zeros_like(gram_sum)
    for column in range(order):
        known = factor[column, :column]
        pivot = jnp.sqrt(gram_sum[column, column] - jnp.sum(known * known))
        factor = factor.at[column, column].set(pivot)
        if column + 1 < order:
            below = gram_sum[column + 1 :, column] - jnp.dot(
                factor[column + 1 :, :column], known, precision=lax.Precision.HIGHEST
            )
            factor = factor.at[column + 1 :, column].set(below / pivot)
    return factor


def solve_written(factor, right_rows):
    order = factor.shape[0]
    forward = []
    for row in range(order):
        value = right_rows[row]
        if row > 0:
            value = value - jnp.dot(
                factor[row, :row], jnp.stack(forward), precision=lax.Precision.HIGHEST
            )
        forward.append(value / factor[row, row])
    backward = [None] * order
    for row in range(order - 1, -1, -1):
        value = forward[row]
        if row < order - 1:
            later = jnp.stack(backward[row + 1 :])
            value = value - jnp.dot(factor[row + 1 :, row], later, precision=lax.Precision.HIGHEST)
        backward[row] = value / factor[row, row]
    return jnp.stack(backward)


def solve_normal(gram_sum, cross_sum):
    order = gram_sum.shape[0]
    factor = factor_lower(gram_sum)
    inverse = solve_written(factor, jnp.eye(order, dtype=jnp.float32))
    return jnp.einsum("kj,cjg->ckg", inverse, cross_sum, precision=lax.Precision.HIGHEST)


def association_block(residual, dosage, windows, first_snp):
    window_len = windows.shape[1]
    every_snp = jnp.einsum(
        "sd,dcg->gsc", dosage.astype(jnp.float32), residual, precision=lax.Precision.HIGHEST
    )
    padded = jnp.pad(every_snp, ((0, 0), (0, window_len), (0, 0)))
    starts = windows[:, 0] - first_snp
    gene_ids = jnp.arange(windows.shape[0], dtype=jnp.int32)

    def one_gene(pair):
        gene_id, start = pair
        gene_rows = lax.dynamic_index_in_dim(padded, gene_id, 0, keepdims=False)
        return lax.dynamic_slice_in_dim(gene_rows, start, window_len, 0)

    sliced = lax.map(one_gene, (gene_ids, starts))
    products = jnp.transpose(sliced, (2, 0, 1))
    scaling = 1.0 / math.sqrt(dosage.shape[1])
    return jnp.where((windows >= 0)[None], products, 0.0) * scaling


def owner_index(cell_donor, cell_type, donors_here, groups):
    cell_slot = cell_donor // (donors_here * groups)
    local_donor = cell_slot * donors_here + cell_donor % donors_here
    return jnp.where(cell_type >= 0, local_donor * CT + cell_type, -1)


def per_device(counts, cell_donor, cell_type, covariates, dosage, windows):
    groups = lax.axis_size("donor")
    donors_here = covariates.shape[0]
    cell_count = counts.shape[0]
    owner_slot = owner_index(cell_donor, cell_type, donors_here, groups)
    counts_half = counts.astype(jnp.bfloat16)
    first_snp = lax.axis_index("gene") * dosage.shape[0]
    row_ids = lax.broadcasted_iota(
        jnp.int32, (donors_here * CT * lax.axis_size("cell"), cell_count), 0
    )
    onehot_table = (row_ids == owner_slot[None, :]).astype(jnp.bfloat16)
    pseudobulk = lax.psum_scatter(
        jnp.dot(onehot_table, counts_half, preferred_element_type=jnp.float32),
        "cell",
        scatter_dimension=0,
        tiled=True,
    )
    library = lax.psum(jnp.sum(pseudobulk, axis=1), "gene")
    expression = log_cpm(pseudobulk, library[:, None]).reshape(donors_here, CT, -1)
    design = with_intercept(covariates)
    gram_part = jnp.dot(design.T, design, precision=lax.Precision.HIGHEST)
    cross_part = jnp.einsum("dk,dcg->ckg", design, expression, precision=lax.Precision.HIGHEST)
    gram_sum, cross_sum = lax.psum((gram_part, cross_part), ("cell", "donor"))
    coefficients = solve_normal(gram_sum, cross_sum)
    residual = expression - jnp.einsum(
        "dk,ckg->dcg", design, coefficients, precision=lax.Precision.HIGHEST
    )
    regrouped = lax.all_to_all(residual, ("cell", "donor"), split_axis=2, concat_axis=0, tiled=True)
    return association_block(regrouped, dosage, windows, first_snp)


def solution(mesh):
    in_specs = (
        P(("cell", "donor"), "gene"),
        P(("cell", "donor")),
        P(("cell", "donor")),
        P(("cell", "donor"), None),
        P("gene", None),
        P(("gene", "cell", "donor"), None),
    )
    out_specs = P(None, ("gene", "cell", "donor"), None)
    return jax.shard_map(
        per_device, mesh=mesh, in_specs=in_specs, out_specs=out_specs, check_vma=False
    )
```

profile of v0, /device:TPU:1, one launch (start us, length us, event | category | flops | bytes accessed | tf_op | source)
XLA Modules:
  0.0 813.1 jit_solution(3078640551746485459)
XLA Ops:
  7.3 2.8 fusion
  10.5 252.7 %psum.23 = f32[51,51]{1,0:T(8,128)S(1)} all-reduce(f32[51,51]{1,0:T(8,128)S(1)} %fusion.449), channel_id=1, replica_groups=mesh['cell'=8,'donor'=8,'gene'=8] {'cell','donor'}, use_global_device_ids=true, to_apply=%region_4.5 | all-reduce | flops 2601 | bytes 20808 | tf_op jit(solution)/shard_map/psum | solution.py:109
  375.8 11.7 %scatter.456 = f32[51,51]{1,0:T(8,128)S(1)} dynamic-update-slice(f32[51,51]{1,0:T(8,128)S(1)} %copy.362, f32[1,1]{1,0:T(1,128)} %bitcast.220, s32[]{:T(128)} %constant.2846.clone.1, s32[]{:T(128)} %constant.2846.clone.1) | dynamic-update-slice | bytes 12 | tf_op jit(solution)/shard_map/scatter | solution.py:25
  431.1 1.8 fusion.481
  497.7 0.8 fusion.295
  510.8 0.8 fusion.321
  517.2 1.0 reduce_sum.454
  518.2 14.1 %psum.21 = f32[192]{0:T(256)S(1)} all-reduce(f32[192]{0:T(256)S(1)} %reduce_sum.454), channel_id=1, replica_groups=mesh['cell'=8,'donor'=8,'gene'=8] {'gene'}, use_global_device_ids=true, to_apply=%region_2.3 | all-reduce | flops 192 | bytes 1536 | tf_op jit(solution)/shard_map/psum | solution.py:104
  532.3 1.0 log_multiply_fusion
  533.3 2.5 convolution_bitcast_fusion.1
  537.1 1.4 fusion.335
  539.7 193.4 %all-reduce.5.cloned.1.call-done = f32[24,51,256]{2,1,0:T(8,128)} async-done(((f32[24,51,256]{2,1,0:T(8,128)}), f32[24,51,256]{2,1,0:T(8,128)}) %all-reduce.5.cloned.1.call-update) | async-done | bytes 1253392 | tf_op jit(solution)/shard_map/psum | solution.py:109
  733.0 2.6 convolution_bitcast_fusion
  736.9 1.5 reshape.3475
  738.4 9.8 %all-to-all-start = ((f32[64,1,768]{2,1,0:T(1,128)}), f32[64,1,768]{2,1,0:T(1,128)S(1)}, u32[]{:S(2)}, u32[]{:S(2)}) async-start(f32[64,1,768]{2,1,0:T(1,128)} %reshape.3475), calls=%async_computation.1 | async-start | bytes 393216 | tf_op jit(solution)/shard_map/all_to_all | solution.py:114
  748.3 11.7 %all-to-all-done = f32[64,1,768]{2,1,0:T(1,128)S(1)} async-done(((f32[64,1,768]{2,1,0:T(1,128)}), f32[64,1,768]{2,1,0:T(1,128)S(1)}, u32[]{:S(2)}, u32[]{:S(2)}) %all-to-all-start) | async-done | bytes 196640 | tf_op jit(solution)/shard_map/all_to_all | solution.py:114
  760.6 1.2 reduce.398
  762.6 6.8 fusion.5
  769.4 34.5 %while.115 = (s32[]{:T(128)}, f32[4,1024,24]{1,0,2:T(4,128)}, s32[4]{0:T(128)S(1)}, s32[4]{0:T(128)S(1)}, f32[4,2048,24]{1,2,0:T(8,128)S(1)}) while((s32[]{:T(128)}, f32[4,1024,24]{1,0,2:T(4,128)}, s32[4]{0:T(128)S(1)}, s32[4]{0:T(128)S(1)}, f32[4,2048,24]{1,2,0:T(8,128)S(1)}) %tuple.543), condition=%wide.region_55.56_spmd.clone, body=%wide.region_54.55_spmd.sunk.clone | while | flops 10 | bytes 590021 | solution.py:75
  775.1 2.9 dynamic_update_slice.10
  783.8 2.9 dynamic_update_slice.10
  792.4 2.9 dynamic_update_slice.10
  801.0 2.9 dynamic_update_slice.10
  803.9 1.9 multiply_bitcast_fusion
  (625 shorter events, 181.2 us)
Async XLA Ops:
  6.5 510.6 %reduce-scatter.2.cloned.1.call-start = ((), (), s32[]{:S(2)}) async-start(), calls=%async_computation.2 | async-start | bytes 1769472 | tf_op jit(solution)/shard_map/reduce_scatter | solution.py:98
  7.2 2.9 copy-start.1
  10.1 722.9 %all-reduce.5.cloned.1.call-start = ((), (), s32[]{:S(2)}) async-start(), calls=%async_computation.3 | async-start | bytes 2752512 | tf_op jit(solution)/shard_map/psum | solution.py:109
  736.4 11.7 %copy-start.2 = (s32[4,1024]{1,0:T(4,128)S(1)}, s32[4,1024]{1,0:T(4,128)}, u32[]{:S(2)}) copy-start(s32[4,1024]{1,0:T(4,128)} %param.215) | copy-start | bytes 49156
  736.9 25.7 %copy-start = (s32[1024,512]{1,0:T(8,128)S(1)}, s32[1024,512]{1,0:T(8,128)}, u32[]{:S(2)}) copy-start(s32[1024,512]{1,0:T(8,128)} %param.214) | copy-start | bytes 6291460
  738.4 21.7 %all-to-all-start = ((f32[64,1,768]{2,1,0:T(1,128)}), f32[64,1,768]{2,1,0:T(1,128)S(1)}, u32[]{:S(2)}, u32[]{:S(2)}) async-start(f32[64,1,768]{2,1,0:T(1,128)} %reshape.3475), calls=%async_computation.1 | async-start | bytes 393216 | tf_op jit(solution)/shard_map/all_to_all | solution.py:114
Sparse Core Ops, SparseCore 0:
  10.3 45.2 reduce-scatter.1
  535.9 197.0 all-reduce.4
where the time goes:
time: 824 us; the launch traced here: 813 us
  blocking collectives  267 us (32%)
  waiting for transfers between devices  205 us (25%)
  matrix products  96.3 us (12%)
  local copies, waits for them, and re-layouts  94.6 us (11%)
  between operations  84 us (10%)
  other arithmetic  39.8 us (5%)
  loops' own time  16.7 us (2%)
  starting transfers between devices  9.82 us (1%)
    psum x1, blocking collectives, per_device(): gram_sum, cross_sum = lax.psum((gram_part, cross_part), ('cell', 'donor'))  253 us
    psum x1, waiting for transfers between devices, per_device(): gram_sum, cross_sum = lax.psum((gram_part, cross_part), ('cell', 'donor'))  193 us
    dot_general x49, matrix products, solve_written(): jnp.dot(factor[row + 1:, row], later, precision=lax.Precision.HIGHEST)  37.7 us
    dot_general x49, matrix products, solve_written(): jnp.dot(factor[row, :row], jnp.stack(forward), precision=lax.Precision.HI...  36.4 us
    reduce_sum x49, other arithmetic, factor_lower(): pivot = jnp.sqrt(gram_sum[column, column] - jnp.sum(known * known))  30 us
    scatter x50, local copies, waits for them, and re-layouts, factor_lower(): factor = factor.at[column + 1:, column].set(below / pivot)  19.3 us
    scatter x50, local copies, waits for them, and re-layouts, factor_lower(): factor = factor.at[column, column].set(pivot)  18.7 us
    another operation x1, loops' own time, association_block(): sliced = lax.map(one_gene, (gene_ids, starts))  16.7 us
  transfers between devices with their start and end apart: 3, of which 2 were waited for; matrix products, arithmetic and copies ran while one was open for 23% of the time, Pallas kernels for 0%

commit v1 on v0

--- a/solution.py
+++ b/solution.py
@@ -106,7 +106,7 @@
     design = with_intercept(covariates)
     gram_part = jnp.dot(design.T, design, precision=lax.Precision.HIGHEST)
     cross_part = jnp.einsum("dk,dcg->ckg", design, expression, precision=lax.Precision.HIGHEST)
-    gram_sum, cross_sum = lax.psum((gram_part, cross_part), ("cell", "donor"))
+    gram_sum, cross_sum = lax.psum(lax.psum((gram_part, cross_part), "cell"), "donor")
     coefficients = solve_normal(gram_sum, cross_sum)
     residual = expression - jnp.einsum(
         "dk,ckg->dcg", design, coefficients, precision=lax.Precision.HIGHEST

time: 824 us -> 570 us (0.69)
  blocking collectives: 267 us -> 72.3 us
  waiting for transfers between devices: 205 us -> 156 us
  local copies, waits for them, and re-layouts: 94.6 us -> 85.5 us
    psum x1 -> x2, blocking collectives: 253 us -> 57.9 us  [the longest x1 29.9 us: per_device(): lax.psum((gram_part, cross_part), 'cell')]
    psum x1 -> x2, waiting for transfers between devices: 193 us -> 144 us  [the longest x1 73.7 us: per_device(): lax.psum(lax.psum((gram_part, cross_part), 'cell'), 'donor')]
    dynamic_update_slice x8, local copies, waits for them, and re-layouts: 12.1 us -> 3.65 us  [association_block(): sliced = lax.map(one_gene, (gene_ids, starts))]
  transfers between devices with their start and end apart: 3 -> 4, of which waited for: 2 -> 3; matrix products, arithmetic and copies ran while one was open for 23% -> 34% of each run, Pallas kernels for 0% -> 0%
where the time goes in v1:
time: 570 us; the launch traced here: 559 us
  waiting for transfers between devices  156 us (27%)
  matrix products  95.9 us (17%)
  local copies, waits for them, and re-layouts  85.5 us (15%)
  between operations  83.7 us (15%)
  blocking collectives  72.3 us (13%)
  other arithmetic  38.8 us (7%)
  loops' own time  15.7 us (3%)
  starting transfers between devices  11.4 us (2%)
    psum x1, waiting for transfers between devices, per_device(): lax.psum(lax.psum((gram_part, cross_part), 'cell'), 'donor')  73.7 us
    psum x1, waiting for transfers between devices, per_device(): lax.psum((gram_part, cross_part), 'cell')  70.6 us
    dot_general x49, matrix products, solve_written(): jnp.dot(factor[row + 1:, row], later, precision=lax.Precision.HIGHEST)  37.5 us
    dot_general x49, matrix products, solve_written(): jnp.dot(factor[row, :row], jnp.stack(forward), precision=lax.Precision.HI...  36.3 us
    psum x1, blocking collectives, per_device(): lax.psum((gram_part, cross_part), 'cell')  29.9 us
    reduce_sum x49, other arithmetic, factor_lower(): pivot = jnp.sqrt(gram_sum[column, column] - jnp.sum(known * known))  29.9 us
    psum x1, blocking collectives, per_device(): lax.psum(lax.psum((gram_part, cross_part), 'cell'), 'donor')  28 us
    scatter x50, local copies, waits for them, and re-layouts, factor_lower(): factor = factor.at[column + 1:, column].set(below / pivot)  19.3 us
  transfers between devices with their start and end apart: 4, of which 3 were waited for; matrix products, arithmetic and copies ran while one was open for 34% of the time, Pallas kernels for 0%

profile of v1, /device:TPU:1, one launch (start us, length us, event | category | flops | bytes accessed | tf_op | source)
XLA Modules:
  0.0 559.3 jit_solution(13609755686413058785)
XLA Ops:
  7.3 2.8 fusion
  10.5 29.9 %psum.38 = f32[51,51]{1,0:T(8,128)S(1)} all-reduce(f32[51,51]{1,0:T(8,128)S(1)} %fusion.449), channel_id=1, replica_groups=mesh['cell'=8,'donor'=8,'gene'=8] {'cell'}, use_global_device_ids=true, to_apply=%region_5.6 | all-reduce | flops 2601 | bytes 20808 | tf_op jit(solution)/shard_map/psum | solution.py:109
  40.4 28.0 %psum.39 = f32[51,51]{1,0:T(8,128)S(1)} all-reduce(f32[51,51]{1,0:T(8,128)S(1)} %psum.38), channel_id=1, replica_groups=mesh['cell'=8,'donor'=8,'gene'=8] {'donor'}, use_global_device_ids=true, to_apply=%region_6.7 | all-reduce | flops 2601 | bytes 20808 | tf_op jit(solution)/shard_map/psum | solution.py:109
  181.1 11.7 %scatter.456 = f32[51,51]{1,0:T(8,128)S(1)} dynamic-update-slice(f32[51,51]{1,0:T(8,128)S(1)} %copy.363, f32[1,1]{1,0:T(1,128)} %bitcast.220, s32[]{:T(128)} %constant.2846.clone.1, s32[]{:T(128)} %constant.2846.clone.1) | dynamic-update-slice | bytes 12 | tf_op jit(solution)/shard_map/scatter | solution.py:25
  235.3 1.8 fusion.481
  273.9 0.8 fusion.249
  281.1 0.8 fusion.373
  301.0 0.8 fusion.293
  304.1 0.8 fusion.299
  315.0 1.0 reduce_sum.454
  316.0 14.3 %psum.35 = f32[192]{0:T(256)S(1)} all-reduce(f32[192]{0:T(256)S(1)} %reduce_sum.454), channel_id=1, replica_groups=mesh['cell'=8,'donor'=8,'gene'=8] {'gene'}, use_global_device_ids=true, to_apply=%region_2.3 | all-reduce | flops 192 | bytes 1536 | tf_op jit(solution)/shard_map/psum | solution.py:104
  330.4 1.0 log_multiply_fusion
  331.4 2.5 convolution_bitcast_fusion.1
  341.3 70.6 %all-reduce.6.cloned.1.call-done = f32[24,51,256]{2,1,0:T(8,128)} async-done(((f32[24,51,256]{2,1,0:T(8,128)}), f32[24,51,256]{2,1,0:T(8,128)}) %all-reduce.6.cloned.1.call-update) | async-done | bytes 1253392 | tf_op jit(solution)/shard_map/psum | solution.py:109
  413.2 1.4 fusion.335
  415.8 73.7 %all-reduce.8.cloned.1.call-done = f32[24,51,256]{2,1,0:T(8,128)} async-done(((f32[24,51,256]{2,1,0:T(8,128)}), f32[24,51,256]{2,1,0:T(8,128)}) %all-reduce.8.cloned.1.call-update) | async-done | bytes 1253392 | tf_op jit(solution)/shard_map/psum | solution.py:109
  489.4 2.6 convolution_bitcast_fusion
  493.3 1.5 reshape.3475
  494.7 11.1 %all-to-all-start = ((f32[64,1,768]{2,1,0:T(1,128)}), f32[64,1,768]{2,1,0:T(1,128)S(1)}, u32[]{:S(2)}, u32[]{:S(2)}) async-start(f32[64,1,768]{2,1,0:T(1,128)} %reshape.3475), calls=%async_computation.1 | async-start | bytes 393216 | tf_op jit(solution)/shard_map/all_to_all | solution.py:114
  506.0 11.7 %all-to-all-done = f32[64,1,768]{2,1,0:T(1,128)S(1)} async-done(((f32[64,1,768]{2,1,0:T(1,128)}), f32[64,1,768]{2,1,0:T(1,128)S(1)}, u32[]{:S(2)}, u32[]{:S(2)}) %all-to-all-start) | async-done | bytes 196640 | tf_op jit(solution)/shard_map/all_to_all | solution.py:114
  518.4 1.1 reduce.398
  520.3 6.6 %fusion.5 = f32[4,1024,24]{1,2,0:T(8,128)S(1)} fusion(s32[1024,512]{1,0:T(8,128)S(1)} %copy-done, f32[64,8,24,4]{2,1,3,0:T(8,128)S(1)} %bitcast.2482), kind=kOutput, calls=%fused_computation.9 | convolution fusion | flops 604504064 | bytes 2686976 | tf_op jit(solution)/shard_map/sd,dcg->gsc/dot_general | solution.py:63
  527.0 24.4 %while.115 = (s32[]{:T(128)}, f32[4,1024,24]{1,0,2:T(4,128)S(1)}, s32[4]{0:T(128)S(1)}, s32[4]{0:T(128)S(1)}, f32[4,2048,24]{1,2,0:T(8,128)S(1)}) while((s32[]{:T(128)}, f32[4,1024,24]{1,0,2:T(4,128)S(1)}, s32[4]{0:T(128)S(1)}, s32[4]{0:T(128)S(1)}, f32[4,2048,24]{1,2,0:T(8,128)S(1)}) %tuple.552), condition=%wide.region_57.58_spmd.clone, body=%wide.region_56.57_spmd.sunk.clone | while | flops 10 | bytes 590021 | solution.py:75
  551.5 0.9 multiply_bitcast_fusion
  (631 shorter events, 182.2 us)
Async XLA Ops:
  6.5 308.5 %reduce-scatter.2.cloned.1.call-start = ((), (), s32[]{:S(2)}) async-start(), calls=%async_computation.2 | async-start | bytes 1769472 | tf_op jit(solution)/shard_map/reduce_scatter | solution.py:98
  7.2 2.9 copy-start.2
  10.1 401.8 %all-reduce.6.cloned.1.call-start = ((), (), s32[]{:S(2)}) async-start(), calls=%async_computation.3 | async-start | bytes 2752512 | tf_op jit(solution)/shard_map/psum | solution.py:109
  333.9 155.5 %all-reduce.8.cloned.1.call-start = ((), (), s32[]{:S(2)}) async-start(), calls=%async_computation.4 | async-start | bytes 2752512 | tf_op jit(solution)/shard_map/psum | solution.py:109
  492.8 13.1 %copy-start.3 = (s32[4,1024]{1,0:T(4,128)S(1)}, s32[4,1024]{1,0:T(4,128)}, u32[]{:S(2)}) copy-start(s32[4,1024]{1,0:T(4,128)} %param.215) | copy-start | bytes 49156
  493.3 27.0 %copy-start = (s32[1024,512]{1,0:T(8,128)S(1)}, s32[1024,512]{1,0:T(8,128)}, u32[]{:S(2)}) copy-start(s32[1024,512]{1,0:T(8,128)} %param.214) | copy-start | bytes 6291460
  494.7 23.0 %all-to-all-start = ((f32[64,1,768]{2,1,0:T(1,128)}), f32[64,1,768]{2,1,0:T(1,128)S(1)}, u32[]{:S(2)}, u32[]{:S(2)}) async-start(f32[64,1,768]{2,1,0:T(1,128)} %reshape.3475), calls=%async_computation.1 | async-start | bytes 393216 | tf_op jit(solution)/shard_map/all_to_all | solution.py:114
  520.3 6.7 %copy-start.1 = (f32[4,1024,24]{1,0,2:T(4,128)S(1)}, f32[4,1024,24]{1,0,2:T(4,128)}, u32[]{:S(2)}) copy-start(f32[4,1024,24]{1,0,2:T(4,128)} %custom-call) | copy-start | bytes 1179652
Sparse Core Ops, SparseCore 0:
  10.3 45.4 reduce-scatter.1
  334.0 77.8 all-reduce.5
  414.4 74.9 all-reduce.7
